TPU v7x, 256 devices: a whole 4x4x8 slice. The times are simulated.
256 devices in a mesh: solver: 2 (over y_lo), gy: 16 (over y_hi, x, core), gz: 8 (over z).
Axes of the slice: x: 4, y: 4 (y_hi: 2, y_lo: 2; y = y_hi * 2 + y_lo), z: 8, core: 2. Of those that a mesh axis runs over, the one named last changes fastest.
Arguments:
- coupled_state: float32 [2, 190, 16, 8, 2048], P('solver', None, 'gy', 'gz'), may hold values from -0.5 to 2.5, as said below
- solid_mask: int32 [5, 16, 8, 2048], P(None, 'gy', 'gz'), may hold values 0 or 1
- inlet_source: int32 [8, 256], P('gz'), may hold values from 0 to 255, as said below
Outputs:
- new_state: float32 [2, 190, 16, 8, 2048], P('solver', None, 'gy', 'gz')
Inputs may be any that keep to these rules, and one draw needn't show every extreme that they name: Block 0 of coupled_state is positive. For every k, inlet_source[k] is a permutation of the 256 rows. Within one k, each outlet tile of 16 rows sends 2 rows to exactly one inlet tile, none to exactly one other, and 1 to each of the rest.
All inputs are finite; a program needn't handle non-finite values. No bound on the sum of `solid_mask` on one device may be relied on, other than what follows from the above.
Results may differ from a plain program's by a relative error of at most 0.0003.
Values sent between devices are 32-bit elements; how exact they have to be, the bound alone decides.
A program may use at most 128 MiB of HBM per device.

v0:
```python
import math

import jax
import jax.numpy as jnp
from jax import lax
from jax.experimental import pallas as pl
from jax.experimental.pallas import tpu as pltpu
from jax.sharding import PartitionSpec as P

CY = 16
CZ = 128
LX = 5
FX = 38
N_GY = 16
N_GZ = 8
MESH = pl.DeviceIdType.MESH
F32 = jnp.float32

VELOCITY_TABLE = [
    (0, 0, 0),
    (1, 0, 0),
    (-1, 0, 0),
    (0, 1, 0),
    (0, -1, 0),
    (0, 0, 1),
    (0, 0, -1),
    (1, 1, 0),
    (-1, -1, 0),
    (1, -1, 0),
    (-1, 1, 0),
    (1, 0, 1),
    (-1, 0, -1),
    (1, 0, -1),
    (-1, 0, 1),
    (0, 1, 1),
    (0, -1, -1),
    (0, 1, -1),
    (0, -1, 1),
]
OPPOSITE_TABLE = [0, 2, 1, 4, 3, 6, 5, 8, 7, 10, 9, 12, 11, 14, 13, 16, 15, 18, 17]
RELAX_TIME = 0.8
SURF_TENSION = 0.02
SEGREGATION_BETA = 0.7
GRAD_FLOOR = 0.1
TIME_STEP = 0.2
VISCOSITY = 0.05
DIFFUSION = 0.05
DENSITY_LOG = math.log(2.0)

PLUS_Z = [i for i in range(19) if VELOCITY_TABLE[i][2] == 1]
MINUS_Z = [i for i in range(19) if VELOCITY_TABLE[i][2] == -1]
PLUS_Y = [i for i in range(19) if VELOCITY_TABLE[i][1] == 1]
SIGNS = (0, 1, -1)
CLASSES = [
    [i for i in range(19) if VELOCITY_TABLE[i][1:] == (sy, sz)] for sy in SIGNS for sz in SIGNS
]
MINUS_Y = [i for i in range(19) if VELOCITY_TABLE[i][1] == -1]

GROUP = 6
N_GROUPS = 7
LAST_ROWS = FX - GROUP * (N_GROUPS - 1)
CHUNKS = (
    ((6, LAST_ROWS), (5, GROUP)),
    ((4, GROUP), (3, GROUP)),
    ((2, GROUP), (1, GROUP)),
    ((0, GROUP),),
)


ROUTE_ROWS = 8 * N_GY
PIPE_ROWS = 2 * (2 * 2 * 5 * FX + 2 * CY * N_GROUPS)
FACE_ROWS = 2 * 2 * CY + 2 * 3 * 16 + 2 * 2 * 16
CORNER_ROWS = 4 * 2 * 8 + 4 * 16
POP_ROWS = 2 * 5 * 2
NOZZLE_ROWS = 4 * (FACE_ROWS + CORNER_ROWS) + POP_ROWS * 2 * (LX + 1)
MOST_ROWS = ROUTE_ROWS + max(PIPE_ROWS, NOZZLE_ROWS)


def weighted_sum(values):
    faces = values[1]
    for i in range(2, 7):
        faces = faces + values[i]
    edges = values[7]
    for i in range(8, 19):
        edges = edges + values[i]
    return values[0] * (1.0 / 3.0) + faces * (1.0 / 18.0) + edges * (1.0 / 36.0)


def clip_row(row):
    return min(max(row, 0), LX) if isinstance(row, int) else jnp.clip(row, 0, LX)


def weight_of(i):
    return 1.0 / 3.0 if i == 0 else (1.0 / 18.0 if i < 7 else 1.0 / 36.0)


def part_sum(directions, read):
    total = None
    for weight in (1.0 / 3.0, 1.0 / 18.0, 1.0 / 36.0):
        values = [read(i) for i in directions if weight_of(i) == weight]
        if values:
            group = values[0]
            for value in values[1:]:
                group = group + value
            total = weight * group if total is None else total + weight * group
    return total


def weighted_momentum(values, dim):
    faces = None
    edges = None
    for i in range(1, 19):
        sign = VELOCITY_TABLE[i][dim]
        if sign == 0:
            continue
        if i < 7:
            faces = (
                values[i]
                if faces is None
                else (faces + values[i] if sign > 0 else faces - values[i])
            )
        else:
            edges = (
                values[i]
                if edges is None
                else (edges + values[i] if sign > 0 else edges - values[i])
            )
    return faces * (1.0 / 18.0) + edges * (1.0 / 36.0)


def along(direction, vec):
    total = None
    for sign, part in zip(VELOCITY_TABLE[direction], vec):
        if sign == 0:
            continue
        if total is None:
            total = part if sign > 0 else -part
        else:
            total = total + part if sign > 0 else total - part
    return total


def equilibrium_list(density, vec):
    speed_sq = vec[0] * vec[0] + vec[1] * vec[1] + vec[2] * vec[2]
    rest = density * (1.0 - 1.5 * speed_sq)
    out = [rest]
    for i in range(1, 19, 2):
        proj = along(i, vec)
        even = rest + (4.5 * density) * (proj * proj)
        odd = (3.0 * density) * proj
        out += [even + odd, even - odd]
    return out


def read_moved(moved, colour, i, x):
    return moved[colour, i, clip_row(x - VELOCITY_TABLE[i][0])]


def relax_cells(x, moved, masses, relaxed):
    for i, value in enumerate(relaxed_list(x, moved, masses)):
        relaxed[i] = value


def relaxed_list(x, moved, masses):
    total = masses[0, x + 1] + masses[1, x + 1]
    inverse = 1.0 / total
    mixed = [read_moved(moved, 0, i, x) + read_moved(moved, 1, i, x) for i in range(19)]
    vec = [weighted_momentum(mixed, dim) * inverse for dim in range(3)]
    balance = equilibrium_list(total, vec)
    return [m - (m - b) * (1.0 / RELAX_TIME) for m, b in zip(mixed, balance)]


def collide_cells(x, moved, masses, slopes, solid_ref, write, relaxed=None):
    def read(colour, i):
        return read_moved(moved, colour, i, x)

    red = masses[0, x + 1]
    blue = masses[1, x + 1]
    total = red + blue
    inverse = 1.0 / total
    if relaxed is None:
        settled = relaxed_list(x, moved, masses)
    else:
        settled = [relaxed[i] for i in range(19)]
    grad = [slopes[dim, x] for dim in range(3)]
    grad_sq = grad[0] * grad[0] + grad[1] * grad[1] + grad[2] * grad[2]
    inverse_norm = 1.0 / jnp.sqrt(grad_sq + GRAD_FLOOR * GRAD_FLOOR)
    red_part = red * inverse
    tension = SURF_TENSION * inverse_norm
    level = tension * grad_sq * (1.0 / 3.0)
    split = SEGREGATION_BETA * (red_part * blue) * inverse_norm
    solid = solid_ref[x] != 0
    for i in range(19):
        value = settled[i] - level
        if i:
            slope = along(i, grad)
            value = value + tension * (slope * slope)
            red_value = red_part * value + split * slope
        else:
            red_value = red_part * value
        back = OPPOSITE_TABLE[i]
        red_new = jnp.where(solid, read(0, back), red_value)
        blue_new = jnp.where(solid, read(1, back), value - red_value)
        write(0, i, red_new)
        write(1, i, blue_new)


def kernel(
    pipe_in,
    nozzle_in,
    solid_in,
    inlet_in,
    out_ref,
    moved,
    masses,
    slopes,
    relaxed,
    solid_ref,
    inlet_ref,
    band,
    prof,
    route_out,
    route_in,
    fields_0,
    fields_1,
    zpack,
    zleft,
    zright,
    pops_0,
    pops_1,
    phase_buf,
    ghost_eq,
    own_side,
    class_sums,
    nz_out,
    nz_left,
    nz_right,
    row_sums,
    own_sums,
    row_sums_in,
    row_corners_in,
    own_sums_in,
    tally,
    in_sem,
    send_sem,
    route_recv,
    recv_sem,
):
    solver = lax.axis_index("solver")
    gy = lax.axis_index("gy")
    gz = lax.axis_index("gz")
    other = 1 - solver
    up = lax.rem(gy + 1, N_GY)
    down = lax.rem(gy + N_GY - 1, N_GY)
    right = lax.rem(gz + 1, N_GZ)
    left = lax.rem(gz + N_GZ - 1, N_GZ)
    is_nozzle = solver == 0
    inlet_load = pltpu.make_async_copy(inlet_in, inlet_ref, in_sem.at[1])
    inlet_load.start()
    barrier = pltpu.get_barrier_semaphore()
    for device in (
        (solver, up, gz),
        (solver, down, gz),
        (solver, gy, right),
        (solver, gy, left),
        (solver, up, right),
        (solver, up, left),
        (solver, down, right),
        (solver, down, left),
    ):
        pl.semaphore_signal(barrier, inc=1, device_id=device, device_id_type=MESH)

    def greet(tile, carry):
        pl.semaphore_signal(barrier, inc=1, device_id=(other, tile, gz), device_id_type=MESH)
        return carry

    lax.fori_loop(0, N_GY, greet, 0)

    lane = lax.broadcasted_iota(jnp.int32, (CY, CZ), 1)

    def remote(src, dst, send_sem, recv_sem, device):
        return pltpu.make_async_remote_copy(
            src_ref=src,
            dst_ref=dst,
            send_sem=send_sem,
            recv_sem=recv_sem,
            device_id=device,
            device_id_type=MESH,
        )

    def wait_rows(sem, rows):
        part = tally.at[0:rows, :]
        pltpu.make_async_copy(part, part, sem).wait()

    solid_load = pltpu.make_async_copy(solid_in, solid_ref, in_sem.at[2])
    lane_word = lax.shift_right_logical(lane, 2)

    def pack_word(packed, value, word):
        return jnp.where(lane_word == word, pltpu.roll(value, (4 * word + 2) % CZ, 1), packed)

    def pack_first(group, count):
        packed = jnp.zeros((CY, CZ), F32)
        for row in range(count):
            for field in range(5):
                value = fields_0[field, 2 + GROUP * group + row, 8:24, :]
                packed = pack_word(packed, value, 5 * row + field)
        zpack[0, group] = packed

    def outlet_ghost(fields):
        for field in range(5):
            end = fields[field, 1 + FX, 8:24, :]
            fields[field, 2 + FX, 8:24, :] = end
            fields[field, 3 + FX, 8:24, :] = end

    nozzle_loads = [
        pltpu.make_async_copy(
            nozzle_in.at[:, :, rows, :, :], pops_0.at[:, :, rows, 8:24, :], in_sem.at[k]
        )
        for k, rows in ((0, slice(LX - 1, LX)), (3, slice(0, LX - 1)))
    ]
    pipe_loads = [
        pltpu.make_async_copy(
            pipe_in.at[part, rows, :, :],
            fields_0.at[part, slice(rows.start + 2, rows.stop + 2), 8:24, :],
            in_sem.at[k],
        )
        for k, part, rows in (
            (0, slice(1, 5), slice(0, 1)),
            (2, slice(0, 5), slice(1, FX)),
            (3, slice(0, 1), slice(0, 1)),
        )
    ]

    @pl.when(is_nozzle)
    def _():
        for copy in nozzle_loads:
            copy.start()
        solid_load.start()

    @pl.when(jnp.logical_not(is_nozzle))
    def _():
        for copy in pipe_loads:
            copy.start()

    inlet_load.wait()
    source = inlet_ref[...]
    row_ids = lax.broadcasted_iota(jnp.int32, (1, 256), 1)
    tile_rows = lax.broadcasted_iota(jnp.int32, (N_GY, 256), 0)
    source_tile = lax.shift_right_logical(source, 4)
    target_tile = lax.shift_right_logical(row_ids, 4)
    member = (tile_rows == source_tile).astype(jnp.bfloat16)
    first = lax.broadcasted_iota(jnp.int32, (256, 256), 0)
    second = lax.broadcasted_iota(jnp.int32, (256, 256), 1)
    before = (
        (first < second)
        & (lax.shift_right_logical(first, 4) == lax.shift_right_logical(second, 4))
    ).astype(jnp.bfloat16)
    counts = jnp.dot(member, before, preferred_element_type=F32)
    rank = jnp.sum(counts * member.astype(F32), axis=0, keepdims=True)
    far_tile = jnp.where(is_nozzle, target_tile, source_tile)
    local_row = jnp.where(is_nozzle, source, row_ids)
    mine = (local_row == tile_rows + gy * CY).astype(jnp.bfloat16)
    slot_rows = []
    row_slots = []
    for slot in range(2):
        taken = ((far_tile == tile_rows) & (rank == float(slot))).astype(jnp.bfloat16)
        dims = (((1,), (1,)), ((), ()))
        slot_rows.append(lax.dot_general(taken, mine, dims, preferred_element_type=F32))
        row_slots.append(lax.dot_general(mine, taken, dims, preferred_element_type=F32))

    @pl.when(is_nozzle)
    def _():
        nozzle_loads[0].wait()
        red = [pops_0[0, i, LX - 1, 8:24, :] for i in range(19)]
        blue = [pops_0[1, i, LX - 1, 8:24, :] for i in range(19)]
        red_mass = weighted_sum(red)
        blue_mass = weighted_sum(blue)
        inverse = 1.0 / (red_mass + blue_mass)
        mixed = [r + b for r, b in zip(red, blue)]
        for dim in range(3):
            prof[:, dim * CZ : (dim + 1) * CZ] = weighted_momentum(mixed, dim) * inverse
        prof[:, 3 * CZ :] = (red_mass - blue_mass) * inverse

    @pl.when(jnp.logical_not(is_nozzle))
    def _():
        pipe_loads[0].wait()
        for slot, field in enumerate((4, 1, 2, 3)):
            prof[:, slot * CZ : (slot + 1) * CZ] = fields_0[field, 2, 8:24, :]

    rows = prof[...]
    for slot in range(2):
        picked = jnp.dot(
            slot_rows[slot], rows, precision=lax.Precision.HIGHEST, preferred_element_type=F32
        )
        for part in range(4):
            route_out[:, slot * 4 + part, :] = picked[:, part * CZ : (part + 1) * CZ]

    pl.semaphore_wait(barrier, 8 + N_GY)

    def route(tile):
        return remote(
            route_out.at[tile],
            route_in.at[gy],
            send_sem.at[0],
            route_recv.at[0],
            (other, tile, gz),
        )

    def send_route(tile, carry):
        route(tile).start()
        return carry

    lax.fori_loop(0, N_GY, send_route, 0)

    def take_inflow():
        wait_rows(route_recv.at[0], ROUTE_ROWS)
        total = None
        for slot in range(2):
            arrived = jnp.concatenate(
                [route_in[:, slot * 4 + part, :] for part in range(4)], axis=1
            )
            term = jnp.dot(
                row_slots[slot],
                arrived,
                precision=lax.Precision.HIGHEST,
                preferred_element_type=F32,
            )
            total = term if total is None else total + term
        return [total[:, part * CZ : (part + 1) * CZ] for part in range(4)]

    @pl.when(jnp.logical_not(is_nozzle))
    def _():
        from_left = (lane & 3) < 2

        def group_copies(step, fields, group, count, kinds=range(4)):
            first_row = 2 + GROUP * group
            span = pl.ds(first_row, count)
            arrived = recv_sem.at[4 * step + (N_GROUPS - 1 - group) // 2]
            ends = [
                (fields.at[:, span, 22:24, :], fields.at[:, span, 6:8, :], (solver, up, gz)),
                (fields.at[:, span, 8:10, :], fields.at[:, span, 24:26, :], (solver, down, gz)),
                (zpack.at[step, group], zleft.at[step, group], (solver, gy, right)),
                (zpack.at[step, group], zright.at[step, group], (solver, gy, left)),
            ]
            return [
                remote(ends[k][0], ends[k][1], send_sem.at[0], arrived, ends[k][2]) for k in kinds
            ]

        def send_rows(group, count):
            for copy in group_copies(0, fields_0, group, count, (0, 1)):
                copy.start()

        def send_lanes(group, count):
            pack_first(group, count)
            for copy in group_copies(0, fields_0, group, count, (2, 3)):
                copy.start()

        def split(value):
            high = value.astype(jnp.bfloat16)
            return [high, (value - high.astype(F32)).astype(jnp.bfloat16)]

        def moved_row(fields, along_z, place):
            centre, grad, smooth = [], [], []
            for field in range(5):
                low_x = fields[field, place - 1, 8:24, :]
                high_x = fields[field, place + 1, 8:24, :]
                d_x = (fields[field, place - 2, 8:24, :] - fields[field, place + 2, 8:24, :]) + (
                    8.0 * (high_x - low_x)
                )
                low_y = fields[field, place, 7:23, :]
                high_y = fields[field, place, 9:25, :]
                d_y = (fields[field, place, 6:22, :] - fields[field, place, 10:26, :]) + (
                    8.0 * (high_y - low_y)
                )
                d_z = along_z[field][:, 0:CZ]
                centre.append(fields[field, place, 8:24, :])
                grad.append((d_x, d_y, d_z))
                smooth.append(low_x + high_x + low_y + high_y + along_z[field][:, CZ:])
            scale = TIME_STEP / 12.0
            speed = [scale * centre[k] for k in (1, 2, 3)]
            lift = scale * jnp.exp((1.0 - centre[0]) * DENSITY_LOG)
            spread = TIME_STEP * DIFFUSION
            out = []
            for field in range(4):
                rate = (
                    speed[0] * grad[field][0]
                    + speed[1] * grad[field][1]
                    + speed[2] * grad[field][2]
                )
                if field > 0:
                    rate = rate + lift * grad[4][field - 1]
                out.append((1.0 - 6.0 * spread) * centre[field] + spread * smooth[field] - rate)
            rate = scale * (grad[1][0] + grad[2][1] + grad[3][2])
            out.append((1.0 - 6.0 * spread) * centre[4] + spread * smooth[4] - rate)
            return out

        def run_chunk(step, fields, groups):
            wait_rows(
                recv_sem.at[4 * step + (N_GROUPS - 1 - groups[0][0]) // 2],
                sum(2 * 2 * 5 * count + 2 * CY for _, count in groups),
            )
            lanes_in = []
            for group, count in groups:
                halo = jnp.where(from_left, zleft[step, group], zright[step, group])
                for row in range(count):
                    for field in range(5):
                        here = fields[field, 2 + GROUP * group + row, 8:24, :]
                        edge = pltpu.roll(halo, (-(4 * (5 * row + field) + 2)) % CZ, 1)
                        lanes_in.append(jnp.concatenate(split(here) + split(edge), axis=1))
            lanes_out = jnp.dot(
                jnp.concatenate(lanes_in, axis=0), band[...], preferred_element_type=F32
            )
            done = 0
            for group, count in groups:
                packed = jnp.zeros((CY, CZ), F32)
                for row in range(count):
                    along_z = [lanes_out[(done + k) * CY : (done + k + 1) * CY] for k in range(5)]
                    done += 5
                    place = GROUP * group + row
                    values = moved_row(fields, along_z, 2 + place)
                    for field in range(5):
                        if step == 0:
                            fields_1[field, 2 + place, 8:24, :] = values[field]
                            packed = pack_word(packed, values[field], 5 * row + field)
                        else:
                            out_ref[field * FX + place] = 0.5 * (
                                fields_0[field, 2 + place, 8:24, :] + values[field]
                            )
                if step == 0:
                    zpack[1, group] = packed
                    for copy in group_copies(1, fields_1, group, count):
                        copy.start()

        for copy in pipe_loads[1:]:
            copy.wait()
        send_rows(N_GROUPS - 1, LAST_ROWS)

        def send_step(k, carry):
            send_rows(N_GROUPS - 2 - k, GROUP)
            return carry

        lax.fori_loop(0, N_GROUPS - 1, send_step, 0)
        send_lanes(N_GROUPS - 1, LAST_ROWS)

        def pack_step(k, carry):
            send_lanes(N_GROUPS - 2 - k, GROUP)
            return carry

        lax.fori_loop(0, N_GROUPS - 1, pack_step, 0)
        outlet_ghost(fields_0)
        lane_in = lax.broadcasted_iota(jnp.int32, (CZ, CZ), 0)
        lane_out = lax.broadcasted_iota(jnp.int32, (CZ, CZ), 1)
        ahead = lane_in - lane_out
        wrapped = jnp.where(
            ahead > 64, ahead - CZ, jnp.where(ahead < -64, ahead + CZ, jnp.zeros_like(ahead))
        )
        for part, apart in enumerate((ahead, wrapped)):
            near = (jnp.abs(apart) == 1).astype(F32)
            far = (jnp.abs(apart) == 2).astype(F32)
            slope = jnp.where(apart > 0, 8.0 * near - far, far - 8.0 * near)
            for copy in range(2):
                rows = slice((2 * part + copy) * CZ, (2 * part + copy + 1) * CZ)
                band[rows, 0:CZ] = slope.astype(jnp.bfloat16)
                band[rows, CZ:] = near.astype(jnp.bfloat16)

        run_chunk(0, fields_0, ((6, LAST_ROWS), (5, GROUP)))
        outlet_ghost(fields_1)

        def first_step(k, carry):
            run_chunk(0, fields_0, ((4 - 2 * k, GROUP), (3 - 2 * k, GROUP)))
            return carry

        lax.fori_loop(0, 2, first_step, 0)
        inflow = take_inflow()
        ghost = [0.5 * (1.0 + inflow[3]), inflow[0], inflow[1], inflow[2]]
        for place in range(2):
            for field in range(4):
                fields_0[field, place, 8:24, :] = ghost[field]
                fields_1[field, place, 8:24, :] = ghost[field]
            fields_0[4, place, 8:24, :] = fields_0[4, 2, 8:24, :]
        run_chunk(0, fields_0, ((0, GROUP),))
        for place in range(2):
            fields_1[4, place, 8:24, :] = fields_1[4, 2, 8:24, :]
        run_chunk(1, fields_1, ((6, LAST_ROWS), (5, GROUP)))

        def second_step(k, carry):
            run_chunk(1, fields_1, ((4 - 2 * k, GROUP), (3 - 2 * k, GROUP)))
            return carry

        lax.fori_loop(0, 2, second_step, 0)
        run_chunk(1, fields_1, ((0, GROUP),))

        wait_rows(send_sem.at[0], ROUTE_ROWS + PIPE_ROWS)

    @pl.when(is_nozzle)
    def _():
        def face_copies(step, pops, rows):
            copies = []

            def add(src, dst, device, kind=0):
                arrived = recv_sem.at[2 * step + kind]
                copies.append(remote(src, dst, send_sem.at[0], arrived, device))

            low, high = slice(0, 8), slice(8, 16)
            for k, column, edges in ((0, right, nz_left), (1, left, nz_right)):
                for side, row, part, place in ((0, up, high, 0), (1, down, low, 24)):
                    add(
                        nz_out.at[step, :, part, :],
                        edges.at[step, :, place : place + 8, :],
                        (solver, row, column),
                        1,
                    )
                    add(
                        row_sums.at[step, side, 1 + k],
                        row_corners_in.at[step, side, k],
                        (solver, row, column),
                        1,
                    )
            for i in PLUS_Y:
                add(pops.at[:, i, rows, 23:24, :], pops.at[:, i, rows, 7:8, :], (solver, up, gz))
            for i in MINUS_Y:
                add(pops.at[:, i, rows, 8:9, :], pops.at[:, i, rows, 24:25, :], (solver, down, gz))
            add(row_sums.at[step, 0], row_sums_in.at[step, 0], (solver, up, gz))
            add(row_sums.at[step, 1], row_sums_in.at[step, 1], (solver, down, gz))
            for k, column, edges in ((0, right, nz_left), (1, left, nz_right)):
                add(nz_out.at[step], edges.at[step, :, 8:24, :], (solver, gy, column))
                add(own_sums.at[step, 1 + k], own_sums_in.at[step, k], (solver, gy, column))
            return copies

        def lane_of(directions, i, colour, row):
            return 2 * ((directions.index(i) * 2 + colour) * 6 + row) + (directions is MINUS_Z)

        def ghost_row(pops, phase_last):
            for i in range(19):
                pops[0, i, LX, 8:24, :] = (1.0 + phase_last) * ghost_eq[i]
                pops[1, i, LX, 8:24, :] = (1.0 - phase_last) * ghost_eq[i]

        def pack_faces(pops, rows, packed):
            lane_pair = lax.shift_right_logical(lane, 1)
            for row in rows:
                for colour in range(2):
                    for k in range(5):
                        pair = (k * 2 + colour) * 6 + row
                        value = jnp.where(
                            lane < CZ // 2,
                            pops[colour, MINUS_Z[k], row, 8:24, :],
                            pops[colour, PLUS_Z[k], row, 8:24, :],
                        )
                        value = pltpu.roll(value, 2 * pair + 1, 1)
                        packed = jnp.where(lane_pair == pair, value, packed)
            return packed

        def pack_classes(pops, cells, packed):
            for x in cells:
                for colour in range(2):
                    sums = []
                    for k, directions in enumerate(CLASSES):
                        value = part_sum(
                            directions,
                            lambda i: pops[
                                colour, i, min(max(x - VELOCITY_TABLE[i][0], 0), LX), 8:24, :
                            ],
                        )
                        class_sums[k, colour, x] = value
                        sums.append(value)
                    for k in range(3):
                        word = 10 * k + 5 * colour + x
                        value = jnp.where(
                            lane == 126,
                            sums[3 * k + 1],
                            jnp.where(lane == 1, sums[3 * k + 2], sums[3 * k]),
                        )
                        value = pltpu.roll(value, 4 * word + 2, 1)
                        packed = jnp.where(lane_word == word, value, packed)
            return packed

        def edge_rows(step):
            for colour in range(2):
                span = slice(8 * colour, 8 * colour + 8)
                for k in range(3):
                    row_sums[step, 0, k, span, :] = (
                        class_sums[k, colour, :, 15, :] + class_sums[3 + k, colour, :, 14, :]
                    )
                    row_sums[step, 1, k, span, :] = (
                        class_sums[k, colour, :, 0, :] + class_sums[6 + k, colour, :, 1, :]
                    )
                    own_sums[step, k, 0, span, :] = class_sums[6 + k, colour, :, 0, :]
                    own_sums[step, k, 1, span, :] = class_sums[3 + k, colour, :, 15, :]

        def pack(step, pops, rows, cells, packed):
            nz_out[step, 0] = pack_faces(pops, rows, packed[0])
            nz_out[step, 1] = pack_classes(pops, cells, packed[1])

        def send_faces(step, pops, rows):
            edge_rows(step)
            copies = face_copies(step, pops, rows)
            for copy in copies:
                copy.start()

        def stream_in(step, pops, rows, mass_rows, cells):
            wait_rows(recv_sem.at[2 * step], FACE_ROWS + POP_ROWS * len(rows))
            stream(step, pops, rows, range(15))
            for k in mass_rows:
                mass_part(k)
            for x in cells:
                side_part(pops, x)
            wait_rows(recv_sem.at[2 * step + 1], CORNER_ROWS)
            stream(step, pops, rows, range(15, 19))
            for k in mass_rows:
                mass_rest(k)
            phase_rows(step)

        def stream(step, pops, rows, directions):
            for colour in range(2):
                for i in directions:
                    shift_y, shift_z = VELOCITY_TABLE[i][1:]
                    span = slice(8 - shift_y, 24 - shift_y)
                    for row in rows:
                        value = pops[colour, i, row, span, :]
                        if shift_z == 1:
                            place = lane_of(PLUS_Z, i, colour, row)
                            edge = nz_left[step, 0, span, :]
                            if place:
                                edge = pltpu.roll(edge, CZ - place, 1)
                            value = jnp.where(lane == 0, edge, pltpu.roll(value, 1, 1))
                        elif shift_z == -1:
                            place = lane_of(MINUS_Z, i, colour, row)
                            edge = pltpu.roll(nz_right[step, 0, span, :], CZ - 1 - place, 1)
                            value = jnp.where(lane == CZ - 1, edge, pltpu.roll(value, CZ - 1, 1))
                        moved[colour, i, row] = value


        def read(colour, i, x):
            return read_moved(moved, colour, i, x)

        def mass_part(k):
            for colour in range(2):
                masses[colour, k] = part_sum(range(15), lambda i: read(colour, i, k - 1))

        def mass_rest(k):
            red, blue = (
                masses[colour, k]
                + part_sum(range(15, 19), lambda i: read(colour, i, k - 1))
                for colour in range(2)
            )
            masses[0, k] = red
            masses[1, k] = blue
            phase_buf[k, 8:24, :] = (red - blue) / (red + blue)

        def side_part(pops, x):
            for colour in range(2):

                def shifted(i):
                    shift_x, shift_y = VELOCITY_TABLE[i][0:2]
                    row = clip_row(x - shift_x)
                    return pops[colour, i, row, 8 - shift_y : 24 - shift_y, :]

                low = pltpu.roll(part_sum(MINUS_Z, shifted), CZ - 1, 1)
                high = pltpu.roll(part_sum(PLUS_Z, shifted), 1, 1)
                own_side[colour, x] = jnp.where(lane == CZ - 1, low, high)

        def phase_rows(step):
            for side, place in ((0, 7), (1, 24)):
                part = [row_sums_in[step, side, k] + own_sums[step, k, side] for k in range(3)]
                corner = [
                    row_corners_in[step, side, k] + own_sums_in[step, k, side] for k in range(2)
                ]
                edge_lane = lax.broadcasted_iota(jnp.int32, (16, CZ), 1)
                total = (
                    part[0]
                    + pltpu.roll(jnp.where(edge_lane == CZ - 1, corner[0], part[1]), 1, 1)
                    + pltpu.roll(jnp.where(edge_lane == 0, corner[1], part[2]), CZ - 1, 1)
                )
                red = total[0:8]
                blue = total[8:16]
                phase_buf[1 : 1 + LX, place, :] = ((red - blue) / (red + blue))[0:LX]
        def collide(step, pops, first, last):
            beside = None
            for k, span in enumerate((slice(8, 24), slice(7, 23), slice(9, 25))):
                both = jnp.where(
                    (lane & 3) < 2, nz_left[step, 1, span, :], nz_right[step, 1, span, :]
                )
                beside = both if k == 0 else beside + pltpu.roll(both, CZ - 40 * k, 1)
            beside = beside + jnp.where(
                (lane & 3) < 2, pltpu.roll(beside, 1, 1), pltpu.roll(beside, CZ - 1, 1)
            )

            def side_mass(colour, x):
                far = pltpu.roll(beside, CZ - 2 - 4 * (5 * colour + x), 1)
                return far + own_side[colour, x]

            def slope_step(x):
                here = phase_buf[x + 1, 8:24, :]
                side_red = side_mass(0, x)
                side_blue = side_mass(1, x)
                side = (side_red - side_blue) / (side_red + side_blue)
                low_z = pltpu.roll(jnp.where(lane == CZ - 1, side, here), 1, 1)
                high_z = pltpu.roll(jnp.where(lane == 0, side, here), CZ - 1, 1)
                grad = [
                    0.5 * (phase_buf[x + 2, 8:24, :] - phase_buf[x, 8:24, :]),
                    0.5 * (phase_buf[x + 1, 9:25, :] - phase_buf[x + 1, 7:23, :]),
                    0.5 * (high_z - low_z),
                ]
                for dim in range(3):
                    slopes[dim, x] = grad[dim]

            for x in range(first, last):
                slope_step(x)
            for x in range(first, last if step < 3 else first):

                def write(colour, i, value, x=x):
                    if step < 2:
                        pops_1[colour, i, x, 8:24, :] = value
                    else:
                        out_ref[(19 * colour + i) * LX + x] = value

                ready = relaxed if step == 1 and x == LX - 2 else None
                collide_cells(x, moved, masses, slopes, solid_ref, write, ready)

        empty = (jnp.zeros((CY, CZ), F32), jnp.zeros((CY, CZ), F32))
        nozzle_loads[1].wait()
        solid_load.wait()
        pack(0, pops_0, range(LX), range(LX - 1), empty)
        send_faces(0, pops_0, slice(0, LX))
        inflow = take_inflow()
        outflow = equilibrium_list(jnp.exp(inflow[0]), inflow[1:])
        for i in range(19):
            ghost_eq[i] = 0.5 * outflow[i]
        ghost_row(pops_0, prof[:, 3 * CZ :])
        pack(1, pops_0, (LX,), (LX - 1,), nz_out[0])
        send_faces(1, pops_0, slice(LX, LX + 1))
        stream_in(0, pops_0, range(LX), range(LX), range(LX - 2))
        collide(0, pops_0, 0, LX - 2)
        pack(2, pops_1, range(LX - 2), range(LX - 3), empty)
        send_faces(2, pops_1, slice(0, LX - 2))
        relax_cells(LX - 2, moved, masses, relaxed)
        stream_in(1, pops_0, (LX,), range(LX, LX + 2), range(LX - 2, LX))
        collide(1, pops_0, LX - 2, LX)
        red_last = weighted_sum([pops_1[0, i, LX - 1, 8:24, :] for i in range(19)])
        blue_last = weighted_sum([pops_1[1, i, LX - 1, 8:24, :] for i in range(19)])
        ghost_row(pops_1, (red_last - blue_last) / (red_last + blue_last))
        pack(3, pops_1, range(LX - 2, LX + 1), range(LX - 3, LX), nz_out[2])
        send_faces(3, pops_1, slice(LX - 2, LX + 1))
        stream_in(2, pops_1, range(LX - 2), range(LX - 2), range(LX - 4))
        collide(2, pops_1, 0, LX - 4)
        relax_cells(LX - 4, moved, masses, relaxed)
        stream_in(3, pops_1, range(LX - 2, LX + 1), range(LX - 2, LX + 2), range(LX - 4, LX))
        collide(3, pops_1, LX - 4, LX)
        wait_rows(send_sem.at[0], ROUTE_ROWS + NOZZLE_ROWS)


def finish(done_ref, moved, masses, slopes, relaxed, solid_ref, out_ref, stage, sems):
    is_nozzle = lax.axis_index("solver") == 0

    @pl.when(jnp.logical_not(is_nozzle))
    def _():
        copy = pltpu.make_async_copy(done_ref, out_ref, sems.at[0])
        copy.start()
        copy.wait()

    @pl.when(is_nozzle)
    def _():
        done_pops = done_ref.reshape(2 * 19, LX, CY, CZ)
        out_pops = out_ref.reshape(2 * 19, LX, CY, CZ)
        copies = []
        for x in range(LX):
            row = slice(x, x + 1)

            def write(colour, i, value, x=x):
                stage[19 * colour + i, x] = value

            if x >= LX - 4:
                ready = relaxed if x == LX - 4 else None
                collide_cells(x, moved, masses, slopes, solid_ref, write, ready)
            source = stage if x >= LX - 4 else done_pops
            copies.append(
                pltpu.make_async_copy(
                    source.at[:, row, :, :], out_pops.at[:, row, :, :], sems.at[x]
                )
            )
            copies[-1].start()
        for copy in copies:
            copy.wait()


def on_device(coupled_state, solid_mask, inlet_source):
    words = coupled_state.shape[1]
    vmem = lambda *shape: pltpu.VMEM(shape, F32)
    in_hbm = lambda array: pltpu.with_memory_space_constraint(array, pltpu.HBM)
    dma = lambda *shape: pltpu.SemaphoreType.DMA(shape)
    done = pl.pallas_call(
        kernel,
        out_shape=[
            vmem(words, CY, CZ),
            vmem(2, 19, LX + 1, CY, CZ),
            vmem(2, LX + 2, CY, CZ),
            vmem(3, LX, CY, CZ),
            vmem(19, CY, CZ),
            pltpu.VMEM((LX, CY, CZ), jnp.int32),
        ],
        in_specs=[
            pl.BlockSpec(memory_space=pltpu.HBM),
            pl.BlockSpec(memory_space=pltpu.HBM),
            pl.BlockSpec(memory_space=pltpu.HBM),
            pl.BlockSpec(memory_space=pltpu.HBM),
        ],
        out_specs=[pl.BlockSpec(memory_space=pltpu.VMEM)] * 6,
        scratch_shapes=[
            pltpu.VMEM((1, 256), jnp.int32),
            pltpu.VMEM((512, 256), jnp.bfloat16),
            vmem(CY, 4 * CZ),
            vmem(N_GY, 8, CZ),
            vmem(N_GY, 8, CZ),
            vmem(5, FX + 4, 32, CZ),
            vmem(5, FX + 4, 32, CZ),
            vmem(2, N_GROUPS, CY, CZ),
            vmem(2, N_GROUPS, CY, CZ),
            vmem(2, N_GROUPS, CY, CZ),
            vmem(2, 19, LX + 1, 32, CZ),
            vmem(2, 19, LX + 1, 32, CZ),
            vmem(LX + 2, 32, CZ),
            vmem(19, CY, CZ),
            vmem(2, LX, CY, CZ),
            vmem(9, 2, 8, CY, CZ),
            vmem(4, 2, CY, CZ),
            vmem(4, 2, 32, CZ),
            vmem(4, 2, 32, CZ),
            vmem(4, 2, 3, 16, CZ),
            vmem(4, 3, 2, 16, CZ),
            vmem(4, 2, 3, 16, CZ),
            vmem(4, 2, 2, 16, CZ),
            vmem(4, 2, 2, 16, CZ),
            vmem(MOST_ROWS, CZ),
            dma(4),
            dma(1),
            dma(1),
            dma(8),
        ],
        compiler_params=pltpu.CompilerParams(
            collective_id=0, has_side_effects=True, vmem_limit_bytes=28 << 20
        ),
    )(
        in_hbm(coupled_state.reshape(5, FX, CY, CZ)),
        in_hbm(coupled_state.reshape(2, 19, LX, CY, CZ)),
        in_hbm(solid_mask.reshape(LX, CY, CZ)),
        in_hbm(inlet_source),
    )
    out = pl.pallas_call(
        finish,
        out_shape=pltpu.HBM((words, CY, CZ), F32),
        in_specs=[pl.BlockSpec(memory_space=pltpu.VMEM)] * 6,
        out_specs=pl.BlockSpec(memory_space=pl.ANY),
        scratch_shapes=[vmem(2 * 19, LX, CY, CZ), dma(LX)],
        compiler_params=pltpu.CompilerParams(vmem_limit_bytes=8 << 20),
    )(*(pltpu.with_memory_space_constraint(array, pltpu.VMEM) for array in done))
    return out.reshape(coupled_state.shape)


def solution(mesh):
    return jax.shard_map(
        on_device,
        mesh=mesh,
        in_specs=(P("solver", None, "gy", "gz", None), P(None, "gy", "gz", None), P("gz", None)),
        out_specs=P("solver", None, "gy", "gz", None),
        check_vma=False,
    )
```

profile of v0, /device:TPU:7, one launch (start us, length us, event | category | flops | bytes accessed | tf_op | source)
XLA Modules:
  0.0 26.3 jit_solution(9465341132051901762)
XLA Ops:
  0.0 25.1 %shard_map.37 = (f32[190,16,128]{2,1,0:T(8,128)S(1)}, f32[2,19,6,16,128]{4,3,2,1,0:T(8,128)S(1)}, f32[2,7,16,128]{3,2,1,0:T(8,128)S(1)}, f32[3,5,16,128]{3,2,1,0...) custom-call(f32[5,38,16,128]{3,2,1,0:T(8,128)} %bitcast.4, f32[2,19,5,16,128]{4,3,2,1,0:T(8,128)} %bitcast.5, ...), custom_call_target="tpu_custom_call" | custom-call | tf_op jit(solution)/shard_map/pallas_call | solution.py:891
  25.1 1.2 %shard_map.38 = f32[190,16,128]{2,1,0:T(8,128)} custom-call(f32[190,16,128]{2,1,0:T(8,128)S(1)} %get-tuple-element.11.done_ref, f32[2,19,6,16,128]{4,3,2,1,0:T(8,128)S(1)} %get-tuple-element.12.moved, f32[2,7,16,128]{3,2,1,0:T(8,128)S(1)} %get-tuple-element.13.masses, f32[3,5,16,128]{3,2,1,0:T(8,128)S(1)} %get-tuple-element.14.slopes, ...), custom_call_target="tpu_custom_call" | custom-call | tf_op jit(solution)/shard_map/pallas_call | solution.py:948
where the time goes:
time: 26.4 us; the launch traced here: 26.3 us
  Pallas kernels  26.3 us (100%)
    pallas_call x1, Pallas kernels, on_device(): pl.pallas_call(kernel, out_shape=[vmem(words, CY, CZ), vmem(2, 19, LX + 1...  25.1 us
    pallas_call x1, Pallas kernels, on_device(): pl.pallas_call(finish, out_shape=pltpu.HBM((words, CY, CZ), F32), in_spec...  1.21 us

commit v1 on v0

--- a/solution.py
+++ b/solution.py
@@ -184,7 +184,7 @@
         settled = [relaxed[i] for i in range(19)]
     grad = [slopes[dim, x] for dim in range(3)]
     grad_sq = grad[0] * grad[0] + grad[1] * grad[1] + grad[2] * grad[2]
-    inverse_norm = 1.0 / jnp.sqrt(grad_sq + GRAD_FLOOR * GRAD_FLOOR)
+    inverse_norm = lax.rsqrt(grad_sq + GRAD_FLOOR * GRAD_FLOOR)
     red_part = red * inverse
     tension = SURF_TENSION * inverse_norm
     level = tension * grad_sq * (1.0 / 3.0)

time: 26.4 us -> 26.4 us (level)
  no operation moved by 1% of the time
where the time goes in v1:
time: 26.4 us; the launch traced here: 26.3 us
  Pallas kernels  26.3 us (100%)
    pallas_call x1, Pallas kernels, on_device(): pl.pallas_call(kernel, out_shape=[vmem(words, CY, CZ), vmem(2, 19, LX + 1...  25 us
    pallas_call x1, Pallas kernels, on_device(): pl.pallas_call(finish, out_shape=pltpu.HBM((words, CY, CZ), F32), in_spec...  1.21 us

profile of v1, /device:TPU:7, one launch (start us, length us, event | category | flops | bytes accessed | tf_op | source)
XLA Modules:
  0.0 26.3 jit_solution(13043703923062564411)
XLA Ops:
  0.0 25.0 %shard_map.37 = (f32[190,16,128]{2,1,0:T(8,128)S(1)}, f32[2,19,6,16,128]{4,3,2,1,0:T(8,128)S(1)}, f32[2,7,16,128]{3,2,1,0:T(8,128)S(1)}, f32[3,5,16,128]{3,2,1,0...) custom-call(f32[5,38,16,128]{3,2,1,0:T(8,128)} %bitcast.4, f32[2,19,5,16,128]{4,3,2,1,0:T(8,128)} %bitcast.5, ...), custom_call_target="tpu_custom_call" | custom-call | tf_op jit(solution)/shard_map/pallas_call | solution.py:891
  25.1 1.2 %shard_map.38 = f32[190,16,128]{2,1,0:T(8,128)} custom-call(f32[190,16,128]{2,1,0:T(8,128)S(1)} %get-tuple-element.11.done_ref, f32[2,19,6,16,128]{4,3,2,1,0:T(8,128)S(1)} %get-tuple-element.12.moved, f32[2,7,16,128]{3,2,1,0:T(8,128)S(1)} %get-tuple-element.13.masses, f32[3,5,16,128]{3,2,1,0:T(8,128)S(1)} %get-tuple-element.14.slopes, ...), custom_call_target="tpu_custom_call" | custom-call | tf_op jit(solution)/shard_map/pallas_call | solution.py:948
